TPU v7x, 1024 devices: a whole 8x8x8 slice. The times are simulated.
1024 devices in a mesh: expert: 64 (over y, x), dp: 16 (over z, core).
Axes of the slice: x: 8, y: 8, z: 8, core: 2. Of those that a mesh axis runs over, the one named last changes fastest.
Arguments:
- tokens: bfloat16 [32768, 1024], P(('expert', 'dp')), may hold values from -6 to 6
- out_grad: bfloat16 [32768, 1024], P(('expert', 'dp')), may hold values from -6 to 6
- expert_ids: int32 [32768, 8], P(('expert', 'dp')), may hold values from 0 to 63, all different within a row; in each aligned block of 32 rows (0 to 31, 32 to 63, ...) at most 6 rows name the same one
- gates: bfloat16 [32768, 8], P(('expert', 'dp')), may hold values from 0.019897461 to 0.29882812
- w_gate: bfloat16 [64, 1024, 384], P('expert', 'dp'), may hold values from -0.1875 to 0.1875
- w_up: bfloat16 [64, 1024, 384], P('expert', 'dp'), may hold values from -0.1875 to 0.1875
- w_down: bfloat16 [64, 1024, 384], P('expert', 'dp'), may hold values from -0.3125 to 0.3125
Outputs:
- d_tokens: bfloat16 [32768, 1024], P(('expert', 'dp'))
- d_gates: bfloat16 [32768, 8], P(('expert', 'dp'))
- d_gate_w: float32 [64, 1024, 384], P('expert', 'dp')
- d_up_w: float32 [64, 1024, 384], P('expert', 'dp')
- d_down_w: float32 [64, 1024, 384], P('expert', 'dp')
Inputs may be any that keep to these rules, and one draw needn't show every extreme that they name: `expert_ids`: each row names 8 different experts. The rows of one device (aligned blocks of 32 rows) name no expert more than 6 times, and in every draw some device names some expert exactly 6 times.
All inputs are finite; a program needn't handle non-finite values.
Results may differ from a plain program's by a relative error of at most 0.022.
Values may be sent and summed in bfloat16 or wider, within the bound.
A program may use at most 32 MiB of HBM per device.

v0:
```python
import jax
import jax.numpy as jnp
from jax import lax
from jax.sharding import PartitionSpec as P


def contract_rows(left, right):
    return lax.dot_general(
        left, right, (((0,), (0,)), ((), ())), preferred_element_type=jnp.float32
    )


def per_device(tokens, out_grad, expert_ids, gates, w_gate, w_up, w_down):
    expert_count = lax.axis_size("expert")
    dp_count = lax.axis_size("dp")
    tok_rows, model_dim = tokens.shape
    top_count = expert_ids.shape[1]
    local_experts = w_gate.shape[0]
    hidden_dim = w_gate.shape[2]
    experts = expert_count * local_experts
    capacity = max(2, 3 * tok_rows * top_count // (2 * experts))
    slot_total = experts * capacity
    row_total = expert_count * capacity
    ids_flat = expert_ids.reshape(-1)
    onehot = (ids_flat[:, None] == jnp.arange(experts, dtype=jnp.int32)[None, :]).astype(jnp.int32)
    earlier = jnp.cumsum(onehot, axis=0) - onehot
    slot_pos = jnp.sum(earlier * onehot, axis=1)
    target = ids_flat * capacity + slot_pos
    placed = jnp.arange(slot_total, dtype=jnp.int32)[:, None] == target[None, :]
    place_token = jnp.any(placed.reshape(slot_total, tok_rows, top_count), axis=2).astype(
        jnp.bfloat16
    )
    place_assign = placed.astype(jnp.float32)
    paired = jnp.concatenate([tokens, out_grad], axis=1)
    outgoing = jnp.dot(place_token, paired, preferred_element_type=jnp.float32).astype(jnp.bfloat16)
    out_gates = jnp.dot(place_assign, gates.reshape(-1).astype(jnp.float32)).astype(jnp.bfloat16)
    outgoing = outgoing.reshape(expert_count, local_experts * capacity, 2 * model_dim)
    out_gates = out_gates.reshape(expert_count, local_experts * capacity)
    incoming, in_gates = (
        lax.all_to_all(outgoing, "expert", split_axis=0, concat_axis=0, tiled=True),
        lax.all_to_all(out_gates, "expert", split_axis=0, concat_axis=0, tiled=True),
    )
    incoming = incoming.reshape(expert_count, local_experts, capacity, 2 * model_dim)
    in_gates = in_gates.reshape(expert_count, local_experts, capacity)
    stacked = jnp.concatenate([w_gate, w_up], axis=2)
    stacked_all, down_all = (
        lax.all_gather(stacked, "dp", axis=1, tiled=True),
        lax.all_gather(w_down, "dp", axis=1, tiled=True),
    )
    member = 0
    rows_in = incoming[:, member].reshape(row_total, 2 * model_dim)
    in_rows = rows_in[:, :model_dim]
    grad_rows = rows_in[:, model_dim:]
    gate_rows = in_gates[:, member].reshape(row_total)
    pre_acts = jnp.dot(in_rows, stacked_all[member], preferred_element_type=jnp.float32)
    gate_pre = pre_acts[:, :hidden_dim]
    up_pre = pre_acts[:, hidden_dim:]
    sig_gate = jax.nn.sigmoid(gate_pre)
    act_gate = gate_pre * sig_gate
    hidden = (act_gate * up_pre).astype(jnp.bfloat16)
    expert_out = jnp.einsum(
        "rf,xf->rx", hidden, down_all[member], preferred_element_type=jnp.float32
    )
    gate_score = jnp.sum(grad_rows.astype(jnp.float32) * expert_out, axis=1).astype(jnp.bfloat16)
    scaled = (gate_rows.astype(jnp.float32)[:, None] * grad_rows.astype(jnp.float32)).astype(
        jnp.bfloat16
    )
    hid_grad = jnp.dot(scaled, down_all[member], preferred_element_type=jnp.float32)
    gate_grad = (hid_grad * up_pre * sig_gate * (1.0 + gate_pre * (1.0 - sig_gate))).astype(
        jnp.bfloat16
    )
    up_grad = (hid_grad * act_gate).astype(jnp.bfloat16)
    pair_grad = jnp.concatenate([gate_grad, up_grad], axis=1)
    in_grad = jnp.einsum(
        "rf,xf->rx", pair_grad, stacked_all[member], preferred_element_type=jnp.float32
    )
    inputs_list = [in_rows]
    scaled_list = [scaled]
    hidden_list = [hidden]
    pair_list = [pair_grad]
    returning_list = [in_grad.astype(jnp.bfloat16).reshape(expert_count, capacity, model_dim)]
    score_list = [gate_score.reshape(expert_count, capacity)]
    returning = jnp.stack(returning_list, axis=1).reshape(
        expert_count, local_experts * capacity, model_dim
    )
    scores = jnp.stack(score_list, axis=1).reshape(expert_count, local_experts * capacity)
    home_grad, home_score = (
        lax.all_to_all(returning, "expert", split_axis=0, concat_axis=0, tiled=True),
        lax.all_to_all(scores, "expert", split_axis=0, concat_axis=0, tiled=True),
    )
    d_tokens = contract_rows(place_token, home_grad.reshape(slot_total, model_dim)).astype(
        jnp.bfloat16
    )
    gate_back = contract_rows(place_assign, home_score.reshape(slot_total).astype(jnp.float32))
    d_gates = gate_back.reshape(tok_rows, top_count).astype(jnp.bfloat16)
    shard_rows = model_dim // dp_count
    blocks_out = []
    member = 0
    in_cols = inputs_list[member]
    scaled_cols = scaled_list[member]
    blocks_out.append(contract_rows(in_cols, pair_list[member]))
    blocks_out.append(contract_rows(scaled_cols, hidden_list[member]))
    summed = lax.psum_scatter(
        jnp.concatenate(blocks_out, axis=1).astype(jnp.bfloat16),
        "dp",
        scatter_dimension=0,
        tiled=True,
    ).astype(jnp.float32)
    summed = summed.reshape(shard_rows, local_experts, 3, hidden_dim)
    d_gate_w = jnp.transpose(summed[:, :, 0], (1, 0, 2))
    d_up_w = jnp.transpose(summed[:, :, 1], (1, 0, 2))
    d_down_w = jnp.transpose(summed[:, :, 2], (1, 0, 2))
    return (d_tokens, d_gates, d_gate_w, d_up_w, d_down_w)


def solution(mesh):
    return jax.shard_map(
        per_device,
        mesh=mesh,
        in_specs=(
            P(("expert", "dp"), None),
            P(("expert", "dp"), None),
            P(("expert", "dp"), None),
            P(("expert", "dp"), None),
            P("expert", "dp", None),
            P("expert", "dp", None),
            P("expert", "dp", None),
        ),
        out_specs=(
            P(("expert", "dp"), None),
            P(("expert", "dp"), None),
            P("expert", "dp", None),
            P("expert", "dp", None),
            P("expert", "dp", None),
        ),
        check_vma=False,
    )
```

profile of v0, /device:TPU:6, one launch (start us, length us, event | category | flops | bytes accessed | tf_op | source)
XLA Modules:
  0.0 186.3 jit_solution(5730786837516247889)
XLA Ops:
  7.2 0.8 copy.40
  9.0 0.8 copy.44
  10.2 0.8 all_to_all.21
  10.9 17.2 %all-to-all-start = ((bf16[64,1,6]{2,1,0:T(2,128)(2,1)}), bf16[64,1,6]{2,1,0:T(2,128)(2,1)S(1)}, u32[]{:S(2)}, u32[]{:S(2)}) async-start(bf16[64,1,6]{2,1,0:T(2,128)(2,1)} %all_to_all.21), calls=%async_computation | async-start | bytes 65536 | tf_op jit(solution)/shard_map/all_to_all | solution.py:41
  28.4 1.5 convolution_convert_fusion
  29.9 1.6 reshape.119
  31.5 5.9 %all-to-all-done = bf16[64,1,6]{2,1,0:T(2,128)(2,1)S(1)} async-done(((bf16[64,1,6]{2,1,0:T(2,128)(2,1)}), bf16[64,1,6]{2,1,0:T(2,128)(2,1)S(1)}, u32[]{:S(2)}, u32[]{:S(2)}) %all-to-all-start) | async-done | bytes 800 | tf_op jit(solution)/shard_map/all_to_all | solution.py:41
  37.4 7.3 %all-to-all-start.1 = ((bf16[64,6,2048]{2,1,0:T(8,128)(2,1)}), bf16[64,6,2048]{2,1,0:T(8,128)(2,1)S(1)}, u32[]{:S(2)}, u32[]{:S(2)}) async-start(bf16[64,6,2048]{2,1,0:T(8,128)(2,1)} %reshape.119), calls=%async_computation.1 | async-start | bytes 4194304 | tf_op jit(solution)/shard_map/all_to_all | solution.py:40
  45.5 27.9 %all_gather.6 = bf16[1,1024,384]{2,1,0:T(8,128)(2,1)S(1)} all-gather(bf16[1,64,384]{2,1,0:T(8,128)(2,1)S(1)} %copy-done.2), channel_id=1, replica_groups=mesh['expert'=64,'dp'=16] {'dp'}, dimensions={1}, use_global_device_ids=true | all-gather | bytes 835584 | tf_op jit(solution)/shard_map/all_gather | solution.py:48
  73.7 19.4 %all-to-all-done.1 = bf16[64,6,2048]{2,1,0:T(8,128)(2,1)S(1)} async-done(((bf16[64,6,2048]{2,1,0:T(8,128)(2,1)}), bf16[64,6,2048]{2,1,0:T(8,128)(2,1)S(1)}, u32[]{:S(2)}, u32[]{:S(2)}) %all-to-all-start.1) | async-done | bytes 1572896 | tf_op jit(solution)/shard_map/all_to_all | solution.py:40
  93.1 1.4 reshape_squeeze_reshape.4
  94.5 7.6 %all-gather.2.cloned.1.call-done = bf16[1,1024,768]{2,1,0:T(8,128)(2,1)} async-done(((bf16[1,64,768]{2,1,0:T(8,128)(2,1)}), bf16[1,1024,768]{2,1,0:T(8,128)(2,1)}) %all-gather.2.cloned.1.call-update) | async-done | bytes 1572880 | tf_op jit(solution)/shard_map/all_gather | solution.py:47
  102.1 2.7 %fusion.4 = f32[384,768]{0,1:T(8,128)S(1)} fusion(bf16[1,1024,768]{2,1,0:T(8,128)(2,1)} %all-gather.2.cloned.1.call-done, bf16[384,2048]{1,0:T(8,128)(2,1)} %reshape_squeeze_reshape.4), kind=kOutput, calls=%fused_computation.9 | convolution fusion | flops 603979776 | bytes 3538944 | tf_op jit(solution)/shard_map/dot_general | solution.py:55
  104.8 0.9 multiply_convert_fusion.2
  106.6 1.0 convolution_convert_fusion.1
  107.8 2.6 %copy.54 = bf16[1024,1152]{1,0:T(8,128)(2,1)} copy(bf16[1024,1152]{0,1:T(8,128)(2,1)S(1)} %pad_maximum_fusion) | data formatting | bytes 4718592
  110.4 1.4 copy-done.1
  111.7 0.7 fusion.1
  112.4 0.8 convert_element_type.85
  113.2 12.8 %all-to-all-start.3 = ((bf16[64,1,6]{2,1,0:T(2,128)(2,1)}), bf16[64,1,6]{2,1,0:T(2,128)(2,1)S(1)}, u32[]{:S(2)}, u32[]{:S(2)}) async-start(bf16[64,1,6]{2,1,0:T(2,128)(2,1)} %convert_element_type.85), calls=%async_computation.3 | async-start | bytes 65536 | tf_op jit(solution)/shard_map/all_to_all | solution.py:89
  126.1 2.2 %fusion.6 = bf16[384,1024]{1,0:T(8,128)(2,1)S(1)} fusion(bf16[1,1024,768]{2,1,0:T(8,128)(2,1)} %all-gather.2.cloned.1.call-done, bf16[384,384]{0,1:T(8,128)(2,1)S(1)} %copy-done.8, bf16[384,384]{0,1:T(8,128)(2,1)S(1)} %copy-done.6), kind=kOutput, calls=%fused_computation.11 | convolution fusion | flops 605552640 | bytes 2949120 | tf_op jit(solution)/shard_map/rf,xf->rx/dot_general | solution.py:74
  128.3 1.2 reshape_stack_reshape.4
  129.5 5.7 %all-to-all-done.3 = bf16[64,1,6]{2,1,0:T(2,128)(2,1)S(1)} async-done(((bf16[64,1,6]{2,1,0:T(2,128)(2,1)}), bf16[64,1,6]{2,1,0:T(2,128)(2,1)S(1)}, u32[]{:S(2)}, u32[]{:S(2)}) %all-to-all-start.3) | async-done | bytes 800 | tf_op jit(solution)/shard_map/all_to_all | solution.py:89
  135.3 7.3 %all-to-all-start.2 = ((bf16[64,6,1024]{2,1,0:T(8,128)(2,1)}), bf16[64,6,1024]{2,1,0:T(8,128)(2,1)S(1)}, u32[]{:S(2)}, u32[]{:S(2)}) async-start(bf16[64,6,1024]{2,1,0:T(8,128)(2,1)} %reshape_stack_reshape.4), calls=%async_computation.2 | async-start | bytes 2097152 | tf_op jit(solution)/shard_map/all_to_all | solution.py:88
  142.8 0.8 fusion.17
  144.2 27.4 %all-to-all-done.2 = bf16[64,6,1024]{2,1,0:T(8,128)(2,1)S(1)} async-done(((bf16[64,6,1024]{2,1,0:T(8,128)(2,1)}), bf16[64,6,1024]{2,1,0:T(8,128)(2,1)S(1)}, u32[]{:S(2)}, u32[]{:S(2)}) %all-to-all-start.2) | async-done | bytes 786464 | tf_op jit(solution)/shard_map/all_to_all | solution.py:88
  171.8 0.9 convolution_convert_fusion.3
  172.7 3.2 %reduce-scatter.4.cloned.1.call-done = bf16[64,1152]{1,0:T(8,128)(2,1)} async-done(((bf16[1024,1152]{1,0:T(8,128)(2,1)}), bf16[64,1152]{1,0:T(8,128)(2,1)}) %reduce-scatter.4.cloned.1.call-update) | async-done | bytes 147472
  176.0 1.1 copy.55
  177.1 0.8 copy.56
  177.9 0.8 copy.57
  178.7 0.8 copy.58
  (45 shorter events, 5.0 us)
Async XLA Ops:
  10.9 26.5 %all-to-all-start = ((bf16[64,1,6]{2,1,0:T(2,128)(2,1)}), bf16[64,1,6]{2,1,0:T(2,128)(2,1)S(1)}, u32[]{:S(2)}, u32[]{:S(2)}) async-start(bf16[64,1,6]{2,1,0:T(2,128)(2,1)} %all_to_all.21), calls=%async_computation | async-start | bytes 65536 | tf_op jit(solution)/shard_map/all_to_all | solution.py:41
  31.5 13.2 %copy-start.3 = (bf16[1,64,384]{2,1,0:T(8,128)(2,1)S(1)}, bf16[1,64,384]{2,1,0:T(8,128)(2,1)}, u32[]{:S(2)}) copy-start(bf16[1,64,384]{2,1,0:T(8,128)(2,1)} %param.12) | copy-start | bytes 147460
  31.5 13.3 %copy-start.4 = (bf16[1,64,384]{2,1,0:T(8,128)(2,1)S(1)}, bf16[1,64,384]{2,1,0:T(8,128)(2,1)}, u32[]{:S(2)}) copy-start(bf16[1,64,384]{2,1,0:T(8,128)(2,1)} %param.11) | copy-start | bytes 147460
  31.5 14.0 %copy-start.2 = (bf16[1,64,384]{2,1,0:T(8,128)(2,1)S(1)}, bf16[1,64,384]{2,1,0:T(8,128)(2,1)}, u32[]{:S(2)}) copy-start(bf16[1,64,384]{2,1,0:T(8,128)(2,1)} %param.13) | copy-start | bytes 147460
  37.4 55.6 %all-to-all-start.1 = ((bf16[64,6,2048]{2,1,0:T(8,128)(2,1)}), bf16[64,6,2048]{2,1,0:T(8,128)(2,1)S(1)}, u32[]{:S(2)}, u32[]{:S(2)}) async-start(bf16[64,6,2048]{2,1,0:T(8,128)(2,1)} %reshape.119), calls=%async_computation.1 | async-start | bytes 4194304 | tf_op jit(solution)/shard_map/all_to_all | solution.py:40
  44.7 57.4 %all-gather.2.cloned.1.call-start = ((), (), s32[]{:S(2)}) async-start(), calls=%async_computation.5 | async-start | bytes 1671168 | tf_op jit(solution)/shard_map/all_gather | solution.py:47
  45.5 130.5 %reduce-scatter.4.cloned.1.call-start = ((), (), s32[]{:S(2)}) async-start(), calls=%async_computation.6 | async-start | bytes 2506752
  94.5 10.3 %copy-start = (bf16[384,2048]{1,0:T(8,128)(2,1)S(1)}, bf16[384,2048]{1,0:T(8,128)(2,1)}, u32[]{:S(2)}) copy-start(bf16[384,2048]{1,0:T(8,128)(2,1)} %reshape_squeeze_reshape.4) | copy-start | bytes 4718596
  105.7 0.7 copy-start.5
  105.7 0.9 copy-start.7
  110.3 1.4 copy-start.1
  111.7 14.3 %copy-start.6 = (bf16[384,384]{0,1:T(8,128)(2,1)S(1)}, bf16[384,384]{0,1:T(8,128)(2,1)}, u32[]{:S(2)}) copy-start(bf16[384,384]{0,1:T(8,128)(2,1)} %copy-done.5) | copy-start | bytes 884740
  111.7 14.3 %copy-start.8 = (bf16[384,384]{0,1:T(8,128)(2,1)S(1)}, bf16[384,384]{0,1:T(8,128)(2,1)}, u32[]{:S(2)}) copy-start(bf16[384,384]{0,1:T(8,128)(2,1)} %copy-done.7) | copy-start | bytes 884740
  113.2 22.0 %all-to-all-start.3 = ((bf16[64,1,6]{2,1,0:T(2,128)(2,1)}), bf16[64,1,6]{2,1,0:T(2,128)(2,1)S(1)}, u32[]{:S(2)}, u32[]{:S(2)}) async-start(bf16[64,1,6]{2,1,0:T(2,128)(2,1)} %convert_element_type.85), calls=%async_computation.3 | async-start | bytes 65536 | tf_op jit(solution)/shard_map/all_to_all | solution.py:89
  135.3 36.3 %all-to-all-start.2 = ((bf16[64,6,1024]{2,1,0:T(8,128)(2,1)}), bf16[64,6,1024]{2,1,0:T(8,128)(2,1)S(1)}, u32[]{:S(2)}, u32[]{:S(2)}) async-start(bf16[64,6,1024]{2,1,0:T(8,128)(2,1)} %reshape_stack_reshape.4), calls=%async_computation.2 | async-start | bytes 2097152 | tf_op jit(solution)/shard_map/all_to_all | solution.py:88
Sparse Core Ops, SparseCore 0:
  48.9 53.2 all-gather.1
  110.5 65.4 reduce-scatter.3
where the time goes:
time: 187 us; the launch traced here: 186 us
  waiting for transfers between devices  69.3 us (37%)
  starting transfers between devices  44.6 us (24%)
  blocking collectives  27.9 us (15%)
  local copies, waits for them, and re-layouts  16.7 us (9%)
  between operations  14.3 us (8%)
  matrix products  11.4 us (6%)
  other arithmetic  2.02 us (1%)
    all_gather x1, blocking collectives, per_device(): lax.all_gather(w_down, 'dp', axis=1, tiled=True)  27.9 us
    all_to_all x1, waiting for transfers between devices, per_device(): lax.all_to_all(returning, 'expert', split_axis=0, concat_axis=0, tiled=True)  27.4 us
    all_to_all x1, waiting for transfers between devices, per_device(): lax.all_to_all(outgoing, 'expert', split_axis=0, concat_axis=0, tiled=True)  19.4 us
    all_to_all x1, starting transfers between devices, per_device(): lax.all_to_all(out_gates, 'expert', split_axis=0, concat_axis=0, tiled=True)  17.2 us
    all_to_all x1, starting transfers between devices, per_device(): lax.all_to_all(scores, 'expert', split_axis=0, concat_axis=0, tiled=True)  12.8 us
    unnamed x25, local copies, waits for them, and re-layouts  9.09 us
    all_gather x1, waiting for transfers between devices, per_device(): lax.all_gather(stacked, 'dp', axis=1, tiled=True)  7.63 us
    all_to_all x1, starting transfers between devices, per_device(): lax.all_to_all(outgoing, 'expert', split_axis=0, concat_axis=0, tiled=True)  7.29 us
  transfers between devices with their start and end apart: 6, of which 6 were waited for; matrix products, arithmetic and copies ran while one was open for 7% of the time, Pallas kernels for 0%

commit v1 on v0

v1 whole, which is shorter than its diff:
```python
import functools

import jax
import jax.numpy as jnp
from jax import lax
from jax.experimental import pallas as pl
from jax.experimental.pallas import tpu as pltpu
from jax.sharding import PartitionSpec as P

MESH = pl.DeviceIdType.MESH
LANES = 128


def dot_nn(a, b):
    return lax.dot_general(a, b, (((1,), (0,)), ((), ())), preferred_element_type=jnp.float32)


def dot_nt(a, b):
    return lax.dot_general(a, b, (((1,), (1,)), ((), ())), preferred_element_type=jnp.float32)


def dot_tn(a, b):
    return lax.dot_general(a, b, (((0,), (0,)), ((), ())), preferred_element_type=jnp.float32)


def far_first(line):
    return sorted(range(1, line), key=lambda k: -min(k, line - k))


def kernel(
    line, ring, cap,
    tok_ref, grad_ref, ids_ref, gates_ref, wg_ref, wu_ref, wd_ref,
    dtok_ref, dgate_ref, dwg_ref, dwu_ref, dwd_ref,
    meta, rows1, send2, recv2, wbuf, back_out, back_in, home_out, home_in,
    part, sib, plus_out, plus_in, minus_out, minus_in,
    meta_s, meta_r, one_s, one_r, two_s, two_r, w_s, w_r, ws_s, ws_r,
    back_s, back_r, home_s, home_r, sib_s, sib_r, plus_s, plus_r, minus_s, minus_r,
):
    tok, dim = tok_ref.shape
    top = ids_ref.shape[0]
    hid = wg_ref.shape[1]
    slots = line * cap
    shard = wg_ref.shape[0]

    expert = lax.axis_index("expert")
    dp = lax.axis_index("dp")
    z, c = dp // 2, dp % 2
    stride_a = line - (line - 1) * c
    stride_b = 1 + (line - 1) * c
    y, x = expert // line, expert % line
    a = y * (1 - c) + x * c
    b = x * (1 - c) + y * c

    def on_a(k):
        return (((a + k + line) % line) * stride_a + b * stride_b, dp)

    def on_b(k):
        return (a * stride_a + ((b + k + line) % line) * stride_b, dp)

    def on_z(k):
        return (expert, ((z + k + ring) % ring) * 2 + c)

    sibling = (expert, z * 2 + 1 - c)

    def remote(src, dst, send, recv, target):
        copy = pltpu.make_async_remote_copy(
            src_ref=src, dst_ref=dst, send_sem=send, recv_sem=recv, device_id=target, device_id_type=MESH
        )
        copy.start()
        return copy

    barrier = pltpu.get_barrier_semaphore()
    for k in range(1, line):
        pl.semaphore_signal(barrier, inc=1, device_id=on_a(k), device_id_type=MESH)
        pl.semaphore_signal(barrier, inc=1, device_id=on_b(k), device_id_type=MESH)
    for k in range(1, ring):
        pl.semaphore_signal(barrier, inc=1, device_id=on_z(k), device_id_type=MESH)
    pl.semaphore_signal(barrier, inc=1, device_id=sibling, device_id_type=MESH)

    ids_f = ids_ref[...].astype(jnp.float32)
    gates_f = gates_ref[...].astype(jnp.float32)
    meta[0, :, 0:tok] = jnp.concatenate([ids_f, gates_f], axis=0).astype(jnp.bfloat16)
    meta[0, :, tok:] = jnp.zeros((2 * top, LANES - tok), jnp.bfloat16)
    rows1[0, :, 0:dim] = tok_ref[...]
    rows1[0, :, dim:] = grad_ref[...]
    wbuf[z, c, :, 0:hid] = wg_ref[...]
    wbuf[z, c, :, hid : 2 * hid] = wu_ref[...]
    wbuf[z, c, :, 2 * hid :] = wd_ref[...]

    pl.semaphore_wait(barrier, 2 * (line - 1) + ring)

    pending = []
    metas, ones, weights = {}, {}, {}
    for k in far_first(line):
        metas[k] = remote(meta.at[0], meta.at[k], meta_s.at[k], meta_r.at[k], on_a(k))
    for k in far_first(line):
        ones[k] = remote(rows1.at[0], rows1.at[k], one_s.at[k], one_r.at[k], on_a(k))
    for k in far_first(ring):
        weights[k] = remote(wbuf.at[z, c], wbuf.at[z, c], w_s.at[k], w_r.at[k], on_z(k))
    pending += list(metas.values()) + list(ones.values()) + list(weights.values())

    for k in range(1, line):
        metas[k].wait_recv()
    every = jnp.concatenate([meta[p].astype(jnp.float32)[:, 0:tok] for p in range(line)], axis=1)
    ids_all, gates_all = every[0:top], every[top:]
    total = line * tok
    masks, scales = [], []
    for j in range(line):
        named = (a * stride_a + ((b + j) % line) * stride_b).astype(jnp.float32)
        hit = ids_all == named
        masks.append(jnp.sum(jnp.where(hit, 1.0, 0.0), axis=0, keepdims=True))
        scales.append(jnp.sum(jnp.where(hit, gates_all, 0.0), axis=0, keepdims=True))
    mask = jnp.concatenate(masks, axis=0)
    rows = lax.broadcasted_iota(jnp.int32, (total, total), 0)
    cols = lax.broadcasted_iota(jnp.int32, (total, total), 1)
    earlier = ((rows < cols) & (rows // tok == cols // tok)).astype(jnp.float32).astype(jnp.bfloat16)
    pos = dot_nn(mask.astype(jnp.bfloat16), earlier)
    first = (lax.broadcasted_iota(jnp.int32, (line, total), 1) // tok * cap).astype(jnp.float32)
    place = jnp.where(mask > 0.0, first + pos, -1.0)
    slot_iota = lax.broadcasted_iota(jnp.int32, (slots, total), 0).astype(jnp.float32)
    picks, scaled_picks = [], []
    for j in range(line):
        hit = slot_iota == place[j : j + 1]
        picks.append(jnp.where(hit, 1.0, 0.0).astype(jnp.bfloat16))
        scaled_picks.append(jnp.where(hit, scales[j], 0.0).astype(jnp.bfloat16))

    for k in range(1, line):
        ones[k].wait_recv()
    gathered = rows1[...].reshape(total, 2 * dim)
    twos = {}
    order = far_first(line) + [0]
    half = max(1, line // 2)
    for start in range(0, line, half):
        group = order[start : start + half]
        tok_rows = dot_nn(jnp.concatenate([picks[j] for j in group], axis=0), gathered[:, 0:dim]).astype(jnp.bfloat16)
        grad_rows = dot_nn(jnp.concatenate([scaled_picks[j] for j in group], axis=0), gathered[:, dim:]).astype(
            jnp.bfloat16
        )
        for i, j in enumerate(group):
            there = send2 if j else recv2
            there[j, :, 0:dim] = tok_rows[i * slots : (i + 1) * slots]
            there[j, :, dim:] = grad_rows[i * slots : (i + 1) * slots]
            if j:
                twos[j] = remote(send2.at[j], recv2.at[j], two_s.at[j], two_r.at[j], on_b(j))
    pending += list(twos.values())

    for k in range(1, ring):
        weights[k].wait_recv()
    shared = remote(wbuf.at[:, c], wbuf.at[:, c], ws_s, ws_r, sibling)
    pending.append(shared)
    for j in range(1, line):
        twos[j].wait_recv()
    shared.wait_recv()

    in_rows = recv2[:, :, 0:dim].reshape(line * slots, dim)
    scaled = recv2[:, :, dim:].reshape(line * slots, dim)
    w_gate = wbuf[:, :, :, 0:hid].reshape(dim, hid)
    w_up = wbuf[:, :, :, hid : 2 * hid].reshape(dim, hid)
    w_down = wbuf[:, :, :, 2 * hid :].reshape(dim, hid)
    gate_pre = dot_nn(in_rows, w_gate)
    up_pre = dot_nn(in_rows, w_up)
    hid_grad = dot_nn(scaled, w_down)
    sig = jax.nn.sigmoid(gate_pre)
    act = gate_pre * sig
    hidden = (act * up_pre).astype(jnp.bfloat16)
    score = jnp.sum(hidden.astype(jnp.float32) * hid_grad, axis=1, keepdims=True)
    gate_grad = (hid_grad * up_pre * sig * (1.0 + gate_pre * (1.0 - sig))).astype(jnp.bfloat16)
    up_grad = (hid_grad * act).astype(jnp.bfloat16)

    in_grad = (dot_nt(gate_grad, w_gate) + dot_nt(up_grad, w_up)).astype(jnp.bfloat16)
    lane = lax.broadcasted_iota(jnp.int32, (line * slots, LANES), 1)
    score_lanes = jnp.where(lane == expert, score, 0.0).astype(jnp.bfloat16)
    backs = {}
    for j in order:
        there = back_out if j else back_in
        there[j, :, 0:dim] = in_grad[j * slots : (j + 1) * slots]
        there[j, :, dim:] = score_lanes[j * slots : (j + 1) * slots]
        if j:
            backs[j] = remote(back_out.at[j], back_in.at[j], back_s.at[j], back_r.at[j], on_b(-j))
    pending += list(backs.values())

    ahead, behind = ring // 2, ring - 1 - ring // 2
    targets = sorted(range(-behind, ahead + 1), key=lambda k: (-abs(k), -k))
    pair_grad = jnp.concatenate([gate_grad, up_grad], axis=1)
    sibs = {}
    for i, k in enumerate(targets):
        zt = (z + k + ring) % ring
        cut = pl.ds(pl.multiple_of(zt * (2 * shard), 2 * shard), 2 * shard)
        cut_grad = pl.ds(pl.multiple_of(dim + zt * (2 * shard), 2 * shard), 2 * shard)
        cols_in = recv2[:, :, cut].reshape(line * slots, 2 * shard)
        cols_scaled = recv2[:, :, cut_grad].reshape(line * slots, 2 * shard)
        part[i, :, :, 0 : 2 * hid] = dot_tn(cols_in, pair_grad).astype(jnp.bfloat16).reshape(2, shard, 2 * hid)
        part[i, :, :, 2 * hid :] = dot_tn(cols_scaled, hidden).astype(jnp.bfloat16).reshape(2, shard, hid)
        sibs[k] = remote(part.at[i, 1 - c], sib.at[i], sib_s.at[i], sib_r.at[i], sibling)
    pending += list(sibs.values())

    def chip_sum(k):
        i = targets.index(k)
        sibs[k].wait_recv()
        return part[i, c].astype(jnp.float32) + sib[i].astype(jnp.float32)

    pluses, minuses = {}, {}

    def hop_plus(h):
        value = chip_sum(ahead - h)
        if h:
            pluses[h - 1].wait_recv()
            value = value + plus_in[h - 1].astype(jnp.float32)
        plus_out[h] = value.astype(jnp.bfloat16)
        pluses[h] = remote(plus_out.at[h], plus_in.at[h], plus_s.at[h], plus_r.at[h], on_z(1))

    def hop_minus(h):
        value = chip_sum(h - behind)
        if h:
            minuses[h - 1].wait_recv()
            value = value + minus_in[h - 1].astype(jnp.float32)
        minus_out[h] = value.astype(jnp.bfloat16)
        minuses[h] = remote(minus_out.at[h], minus_in.at[h], minus_s.at[h], minus_r.at[h], on_z(-1))

    homes = {}

    def combine():
        for j in range(1, line):
            backs[j].wait_recv()
        pick = jnp.concatenate(picks, axis=0)
        summed = dot_tn(pick, back_in[...].reshape(line * slots, dim + LANES)).astype(jnp.bfloat16)
        for p in far_first(line) + [0]:
            there = home_out if p else home_in
            there[p] = summed[p * tok : (p + 1) * tok]
            if p:
                homes[p] = remote(home_out.at[p], home_in.at[p], home_s.at[p], home_r.at[p], on_a(-p))

    for h in range(ahead):
        if h == ahead // 2:
            combine()
        hop_plus(h)
        if h < behind:
            hop_minus(h)
    pending += list(homes.values()) + list(pluses.values()) + list(minuses.values())

    for p in range(1, line):
        homes[p].wait_recv()
    back = home_in[0].astype(jnp.float32)
    for p in range(1, line):
        back = back + home_in[p].astype(jnp.float32)
    dtok_ref[...] = back[:, 0:dim].astype(jnp.bfloat16)
    eye = (
        lax.broadcasted_iota(jnp.int32, (LANES, LANES), 0) == lax.broadcasted_iota(jnp.int32, (LANES, LANES), 1)
    ).astype(jnp.float32).astype(jnp.bfloat16)
    by_expert = dot_nt(eye, back[:, dim:].astype(jnp.bfloat16))
    expert_iota = lax.broadcasted_iota(jnp.int32, (LANES, tok), 0)
    chosen = [
        jnp.sum(jnp.where(expert_iota == ids_ref[k : k + 1, :], by_expert, 0.0), axis=0, keepdims=True)
        for k in range(top)
    ]
    dgate_ref[...] = (jnp.concatenate(chosen, axis=0) / gates_f).astype(jnp.bfloat16)

    summed = chip_sum(0)
    pluses[ahead - 1].wait_recv()
    summed = summed + plus_in[ahead - 1].astype(jnp.float32)
    if behind:
        minuses[behind - 1].wait_recv()
        summed = summed + minus_in[behind - 1].astype(jnp.float32)
    dwg_ref[...] = summed[:, 0:hid]
    dwu_ref[...] = summed[:, hid : 2 * hid]
    dwd_ref[...] = summed[:, 2 * hid :]

    for copy in pending:
        copy.wait_send()


def per_device(line, ring, cap, tokens, out_grad, expert_ids, gates, w_gate, w_up, w_down):
    tok, dim = tokens.shape
    top = expert_ids.shape[1]
    _, shard, hid = w_gate.shape
    slots = line * cap
    ahead, behind = ring // 2, ring - 1 - ring // 2
    bf16, f32 = jnp.bfloat16, jnp.float32
    dma = pltpu.SemaphoreType.DMA
    vmem = pl.BlockSpec(memory_space=pltpu.VMEM)
    d_tokens, d_gates, d_gate_w, d_up_w, d_down_w = pl.pallas_call(
        functools.partial(kernel, line, ring, cap),
        out_shape=[
            jax.ShapeDtypeStruct((tok, dim), bf16),
            jax.ShapeDtypeStruct((top, tok), bf16),
            jax.ShapeDtypeStruct((shard, hid), f32),
            jax.ShapeDtypeStruct((shard, hid), f32),
            jax.ShapeDtypeStruct((shard, hid), f32),
        ],
        in_specs=[vmem] * 7,
        out_specs=[vmem] * 5,
        scratch_shapes=[
            pltpu.VMEM((line, 2 * top, LANES), bf16),
            pltpu.VMEM((line, tok, 2 * dim), bf16),
            pltpu.VMEM((line, slots, 2 * dim), bf16),
            pltpu.VMEM((line, slots, 2 * dim), bf16),
            pltpu.VMEM((ring, 2, shard, 3 * hid), bf16),
            pltpu.VMEM((line, slots, dim + LANES), bf16),
            pltpu.VMEM((line, slots, dim + LANES), bf16),
            pltpu.VMEM((line, tok, dim + LANES), bf16),
            pltpu.VMEM((line, tok, dim + LANES), bf16),
            pltpu.VMEM((ring, 2, shard, 3 * hid), bf16),
            pltpu.VMEM((ring, shard, 3 * hid), bf16),
            pltpu.VMEM((ahead, shard, 3 * hid), bf16),
            pltpu.VMEM((ahead, shard, 3 * hid), bf16),
            pltpu.VMEM((max(behind, 1), shard, 3 * hid), bf16),
            pltpu.VMEM((max(behind, 1), shard, 3 * hid), bf16),
            dma((line,)), dma((line,)), dma((line,)), dma((line,)), dma((line,)), dma((line,)),
            dma((ring,)), dma((ring,)), dma(()), dma(()),
            dma((line,)), dma((line,)), dma((line,)), dma((line,)),
            dma((ring,)), dma((ring,)),
            dma((ahead,)), dma((ahead,)), dma((max(behind, 1),)), dma((max(behind, 1),)),
        ],
        compiler_params=pltpu.CompilerParams(
            collective_id=0, has_side_effects=True, vmem_limit_bytes=56 * 1024 * 1024
        ),
        name="expert_backward",
    )(tokens, out_grad, expert_ids.T, gates.T, w_gate[0], w_up[0], w_down[0])
    return d_tokens, d_gates.T, d_gate_w[None], d_up_w[None], d_down_w[None]


def solution(mesh, cap=6):
    experts, groups = mesh.shape["expert"], mesh.shape["dp"]
    line = 1
    while line * line < experts:
        line += 1
    split, both = P("expert", "dp", None), P(("expert", "dp"), None)
    return jax.shard_map(
        functools.partial(per_device, line, groups // 2, cap),
        mesh=mesh,
        in_specs=(both, both, both, both, split, split, split),
        out_specs=(both, both, split, split, split),
        check_vma=False,
    )
```

time: 187 us -> 89.3 us (0.48)
  the two profiles are of different devices: /device:TPU:6 before, /device:TPU:52 now
where the time goes in v1:
time: 89.3 us; the launch traced here: 89 us
  Pallas kernels  83.8 us (94%)
  local copies, waits for them, and re-layouts  4.59 us (5%)
    pallas_call x1, Pallas kernels, per_device(): pl.pallas_call(functools.partial(kernel, line, ring, cap), out_shape=[jax...  83.8 us
    unnamed x13, local copies, waits for them, and re-layouts  4.59 us

profile of v1, /device:TPU:52, one launch (start us, length us, event | category | flops | bytes accessed | tf_op | source)
XLA Modules:
  0.0 89.0 jit_solution(7601729517557107539)
XLA Ops:
  0.6 83.8 %expert_backward.1 = (bf16[32,1024]{1,0:T(8,128)(2,1)}, bf16[8,32]{1,0:T(8,128)(2,1)}, f32[64,384]{1,0:T(8,128)}, f32[64,384]{1,0:T(8,128)}, f32[64,384]{1,0:T(8,128)}) custom-call(bf16[32,1024]{1,0:T(8,128)(2,1)} %tok_ref.1, bf16[32,1024]{1,0:T(8,128)(2,1)} %grad_ref.1, s32[8,32]{1,0:T(8,128)} %bitcast.15, bf16[8,32]{1,0:T(8,128)(2,1)} %bitcast.16, ...), custom_call_target="tpu_custom_call" | custom-call | tf_op jit(solution)/shard_map/expert_backward/pallas_call | solution.py:281
  84.4 0.0 copy-start.2
  84.4 0.0 copy-start.3
  84.4 1.5 %copy.17 = bf16[32,1024]{1,0:T(8,128)(2,1)} copy(bf16[32,1024]{1,0:T(8,128)(2,1)} %get-tuple-element.20) | data formatting | bytes 131072
  85.9 0.0 copy-done.3
  86.0 0.6 copy.18
  86.5 0.0 copy-done.2
  86.5 0.0 copy-start.1
  86.5 0.6 copy.19
  87.2 0.3 copy-done.1
  87.5 0.0 copy-start
  87.5 0.6 copy.20
  88.1 0.3 copy-done
  88.4 0.6 copy.21
Async XLA Ops:
  84.4 2.1 %copy-start.2 = (f32[64,384]{1,0:T(8,128)S(1)}, f32[64,384]{1,0:T(8,128)}, u32[]{:S(2)}) copy-start(f32[64,384]{1,0:T(8,128)} %get-tuple-element.12) | copy-start | bytes 294916
  84.4 1.5 %copy-start.3 = (bf16[8,32]{1,0:T(8,128)(2,1)S(1)}, bf16[8,32]{1,0:T(8,128)(2,1)}, u32[]{:S(2)}) copy-start(bf16[8,32]{1,0:T(8,128)(2,1)} %get-tuple-element.11) | copy-start | bytes 1540
  86.5 0.9 %copy-start.1 = (f32[64,384]{1,0:T(8,128)S(1)}, f32[64,384]{1,0:T(8,128)}, u32[]{:S(2)}) copy-start(f32[64,384]{1,0:T(8,128)} %get-tuple-element.13) | copy-start | bytes 294916
  87.5 0.9 %copy-start = (f32[64,384]{1,0:T(8,128)S(1)}, f32[64,384]{1,0:T(8,128)}, u32[]{:S(2)}) copy-start(f32[64,384]{1,0:T(8,128)} %get-tuple-element.14) | copy-start | bytes 294916

commit v2 on v1

v2 whole, which is shorter than its diff:
```python
import functools

import jax
import jax.numpy as jnp
from jax import lax
from jax.experimental import pallas as pl
from jax.experimental.pallas import tpu as pltpu
from jax.sharding import PartitionSpec as P

MESH = pl.DeviceIdType.MESH
LANES = 128


def dot_nn(a, b):
    return lax.dot_general(a, b, (((1,), (0,)), ((), ())), preferred_element_type=jnp.float32)


def dot_nt(a, b):
    return lax.dot_general(a, b, (((1,), (1,)), ((), ())), preferred_element_type=jnp.float32)


def dot_tn(a, b):
    return lax.dot_general(a, b, (((0,), (0,)), ((), ())), preferred_element_type=jnp.float32)


def split_rows(slots):
    return (0, 16), (16, slots)


def kernel(
    line, ring, cap,
    tok_ref, grad_ref, ids_ref, gates_ref, wg_ref, wu_ref, wd_ref,
    dtok_ref, dgate_ref, dwg_ref, dwu_ref, dwd_ref,
    meta, rows1, send2, recv2, wbuf, acts, back_out, back_in, home_out, home_in,
    part, sib, plus_out, plus_in, minus_out, minus_in,
    meta_s, meta_r, one_s, one_r, two_s, two_r, w_s, w_r, ws_s, ws_r,
    back_s, back_r, home_s, home_r, sib_s, sib_r, plus_s, plus_r, minus_s, minus_r,
):
    tok, dim = tok_ref.shape
    top = ids_ref.shape[0]
    hid = wg_ref.shape[1]
    slots = line * cap
    shard = wg_ref.shape[0]
    parts = split_rows(slots)
    offsets = sorted(range(line), key=lambda k: (min(k, line - k), k))
    place_of = {k: q for q, k in enumerate(offsets)}

    expert = lax.axis_index("expert")
    dp = lax.axis_index("dp")
    z, c = dp // 2, dp % 2
    stride_a = line - (line - 1) * c
    stride_b = 1 + (line - 1) * c
    y, x = expert // line, expert % line
    a = y * (1 - c) + x * c
    b = x * (1 - c) + y * c

    def on_a(k):
        return (((a + k + line) % line) * stride_a + b * stride_b, dp)

    def on_b(k):
        return (a * stride_a + ((b + k + line) % line) * stride_b, dp)

    def z_at(k):
        return (z + k + ring) % ring

    def on_z(k):
        return (expert, z_at(k) * 2 + c)

    sibling = (expert, z * 2 + 1 - c)
    pending = []

    def remote(src, dst, send, recv, target):
        copy = pltpu.make_async_remote_copy(
            src_ref=src, dst_ref=dst, send_sem=send, recv_sem=recv, device_id=target, device_id_type=MESH
        )
        copy.start()
        pending.append(copy)
        return copy

    barrier = pltpu.get_barrier_semaphore()
    for k in range(1, line):
        pl.semaphore_signal(barrier, inc=1, device_id=on_a(k), device_id_type=MESH)
        pl.semaphore_signal(barrier, inc=1, device_id=on_b(k), device_id_type=MESH)
    for k in range(1, ring):
        pl.semaphore_signal(barrier, inc=1, device_id=on_z(k), device_id_type=MESH)
    pl.semaphore_signal(barrier, inc=1, device_id=sibling, device_id_type=MESH)

    ids_f = ids_ref[...].astype(jnp.float32)
    gates_f = gates_ref[...].astype(jnp.float32)
    meta[0, :, 0:tok] = jnp.concatenate([ids_f, gates_f], axis=0).astype(jnp.bfloat16)
    meta[0, :, tok:] = jnp.zeros((2 * top, LANES - tok), jnp.bfloat16)
    rows1[0, :, 0:dim] = tok_ref[...]
    rows1[0, :, dim:] = grad_ref[...]
    wbuf[z, c, :, 0:hid] = wg_ref[...]
    wbuf[z, c, :, hid : 2 * hid] = wu_ref[...]
    wbuf[z, c, :, 2 * hid :] = wd_ref[...]

    pl.semaphore_wait(barrier, 2 * (line - 1) + ring)

    metas, ones, weights, shared = {}, {}, {}, {}
    for q in range(1, line):
        metas[q] = remote(meta.at[0], meta.at[q], meta_s.at[q], meta_r.at[q], on_a(offsets[q]))

    def send_rows(q, source, target, i=0, lanes=(0, 2 * dim)):
        cut = slice(*lanes)
        ones[q, i] = remote(
            rows1.at[source, :, cut], rows1.at[q, :, cut], one_s.at[q, i], one_r.at[q, i], on_a(target)
        )

    def send_weights(key, k, target, rows=(0, shard)):
        i, cut = len(weights), slice(*rows)
        ref = wbuf.at[z_at(-k), c, cut]
        weights[key] = remote(ref, ref, w_s.at[i], w_r.at[i], on_z(target))

    def share(k):
        i = len(shared)
        ref = wbuf.at[z_at(-k), c]
        shared[k] = remote(ref, ref, ws_s.at[i], ws_r.at[i], sibling)

    near = (1, -1, 2, -2)
    for k in near:
        send_rows(place_of[k % line], 0, k)
    for k in near:
        send_weights(k, 0, k)
    share(0)

    for q in range(1, line):
        metas[q].wait_recv()
    every = jnp.concatenate([meta[q].astype(jnp.float32)[:, 0:tok] for q in range(line)], axis=1)
    ids_all, gates_all = every[0:top], every[top:]
    total = line * tok
    masks, scales = [], []
    for j in range(line):
        named = (a * stride_a + ((b + j) % line) * stride_b).astype(jnp.float32)
        hit = ids_all == named
        masks.append(jnp.sum(jnp.where(hit, 1.0, 0.0), axis=0, keepdims=True))
        scales.append(jnp.sum(jnp.where(hit, gates_all, 0.0), axis=0, keepdims=True))
    mask = jnp.concatenate(masks, axis=0)
    rows = lax.broadcasted_iota(jnp.int32, (total, total), 0)
    cols = lax.broadcasted_iota(jnp.int32, (total, total), 1)
    earlier = ((rows < cols) & (rows // tok == cols // tok)).astype(jnp.float32).astype(jnp.bfloat16)
    pos = dot_nn(mask.astype(jnp.bfloat16), earlier)
    first = (lax.broadcasted_iota(jnp.int32, (line, total), 1) // tok * cap).astype(jnp.float32)
    place = jnp.where(mask > 0.0, first + pos, -1.0)
    holds = [(lo // cap, -(-hi // cap)) for lo, hi in parts]
    slot_iota = lax.broadcasted_iota(jnp.int32, (slots, total), 0).astype(jnp.float32)
    picks, scaled_picks = [[], []], [[], []]
    for j in range(line):
        hit = slot_iota == place[j : j + 1]
        pick = jnp.where(hit, 1.0, 0.0)
        scaled_pick = jnp.where(hit, scales[j], 0.0)
        for g, (lo, hi) in enumerate(parts):
            lanes = slice(holds[g][0] * tok, holds[g][1] * tok)
            picks[g].append(pick[lo:hi, lanes].astype(jnp.bfloat16))
            scaled_picks[g].append(scaled_pick[lo:hi, lanes].astype(jnp.bfloat16))
    picks = [jnp.concatenate(p, axis=0) for p in picks]
    scaled_picks = [jnp.concatenate(p, axis=0) for p in scaled_picks]

    twos = {}

    def dispatch(g):
        (lo, hi), (q0, q1) = parts[g], holds[g]
        count = hi - lo
        for col, pick in ((0, picks[g]), (dim, scaled_picks[g])):
            held = rows1[q0:q1, :, col : col + dim].reshape((q1 - q0) * tok, dim)
            out = dot_nn(pick, held).astype(jnp.bfloat16)
            for j in range(line):
                (send2 if j else recv2)[j, lo:hi, col : col + dim] = out[j * count : (j + 1) * count]
        for q in range(1, line):
            j = offsets[q]
            twos[j, g] = remote(
                send2.at[j, lo:hi], recv2.at[j, lo:hi], two_s.at[j, g], two_r.at[j, g], on_b(j)
            )

    for k in (1, -1):
        ones[place_of[k % line], 0].wait_recv()
    dispatch(0)
    for k in (2, -2):
        ones[place_of[k % line], 0].wait_recv()
    send_rows(place_of[3], place_of[2], 1)
    send_rows(place_of[-3 % line], place_of[-2 % line], -1)
    send_rows(place_of[4], place_of[2], 2, 0, (0, dim))
    send_rows(place_of[4], place_of[-2 % line], -2, 1, (dim, 2 * dim))
    for q, i in ((place_of[3], 0), (place_of[-3 % line], 0), (place_of[4], 0), (place_of[4], 1)):
        ones[q, i].wait_recv()
    dispatch(1)

    for k in near:
        weights[k].wait_recv()
    send_weights(3, 2, 1)
    send_weights(-3, -2, -1)
    send_weights(4, 2, 2, (0, shard // 2))
    send_weights(-4, -2, -2, (shard // 2, shard))
    for k in near:
        share(k)
    for k in (3, -3, 4, -4):
        weights[k].wait_recv()
    for k in (3, -3, 4):
        share(k)
    for copy in list(shared.values()):
        copy.wait_recv()

    backs = {}

    def expert_rows(g):
        lo, hi = parts[g]
        count = hi - lo
        in_rows = recv2[:, lo:hi, 0:dim].reshape(line * count, dim)
        scaled = recv2[:, lo:hi, dim:].reshape(line * count, dim)
        w_pair = wbuf[:, :, :, 0 : 2 * hid].reshape(dim, 2 * hid)
        w_down = wbuf[:, :, :, 2 * hid :].reshape(dim, hid)
        pre = dot_nn(in_rows, w_pair)
        gate_pre, up_pre = pre[:, 0:hid], pre[:, hid:]
        hid_grad = dot_nn(scaled, w_down)
        sig = jax.nn.sigmoid(gate_pre)
        act = gate_pre * sig
        hidden = (act * up_pre).astype(jnp.bfloat16)
        score = jnp.sum(hidden.astype(jnp.float32) * hid_grad, axis=1, keepdims=True)
        gate_grad = (hid_grad * up_pre * sig * (1.0 + gate_pre * (1.0 - sig))).astype(jnp.bfloat16)
        up_grad = (hid_grad * act).astype(jnp.bfloat16)
        pair = jnp.concatenate([gate_grad, up_grad], axis=1)
        acts[:, lo:hi, 0 : 2 * hid] = pair.reshape(line, count, 2 * hid)
        acts[:, lo:hi, 2 * hid :] = hidden.reshape(line, count, hid)
        in_grad = dot_nt(pair, w_pair).astype(jnp.bfloat16)
        lane = lax.broadcasted_iota(jnp.int32, (line * count, LANES), 1)
        score_lanes = jnp.where(lane == expert, score, 0.0).astype(jnp.bfloat16)
        for j in offsets:
            there = back_out if j else back_in
            there[j, lo:hi, 0:dim] = in_grad[j * count : (j + 1) * count]
            there[j, lo:hi, dim:] = score_lanes[j * count : (j + 1) * count]
        for j in offsets[1:]:
            backs[j, g] = remote(
                back_out.at[j, lo:hi], back_in.at[j, lo:hi], back_s.at[j, g], back_r.at[j, g], on_b(-j)
            )

    for j in range(1, line):
        twos[j, 0].wait_recv()
    expert_rows(0)
    for j in range(1, line):
        twos[j, 1].wait_recv()
    expert_rows(1)

    ahead, behind = ring // 2, ring - 1 - ring // 2
    targets = sorted(range(-behind, ahead + 1), key=lambda k: (-abs(k), -k))
    pair_grad = acts[:, :, 0 : 2 * hid].reshape(line * slots, 2 * hid)
    hidden = acts[:, :, 2 * hid :].reshape(line * slots, hid)
    sibs = {}
    for i, k in enumerate(targets):
        zt = z_at(k)
        cut = pl.ds(pl.multiple_of(zt * (2 * shard), 2 * shard), 2 * shard)
        cut_grad = pl.ds(pl.multiple_of(dim + zt * (2 * shard), 2 * shard), 2 * shard)
        cols_in = recv2[:, :, cut].reshape(line * slots, 2 * shard)
        cols_scaled = recv2[:, :, cut_grad].reshape(line * slots, 2 * shard)
        part[i, :, :, 0 : 2 * hid] = dot_tn(cols_in, pair_grad).astype(jnp.bfloat16).reshape(2, shard, 2 * hid)
        part[i, :, :, 2 * hid :] = dot_tn(cols_scaled, hidden).astype(jnp.bfloat16).reshape(2, shard, hid)
        sibs[k] = remote(part.at[i, 1 - c], sib.at[i], sib_s.at[i], sib_r.at[i], sibling)

    met = set()

    def chip_sum(k, m):
        i, lanes = targets.index(k), slice(m * hid, (m + 1) * hid)
        if k not in met:
            sibs[k].wait_recv()
            met.add(k)
        return part[i, c, :, lanes].astype(jnp.float32) + sib[i, :, lanes].astype(jnp.float32)

    pluses, minuses = {}, {}

    def hop(h, m, k, done, out, inn, send, recv, way):
        value = chip_sum(k, m)
        if h:
            done[h - 1, m].wait_recv()
            value = value + inn[h - 1, m].astype(jnp.float32)
        out[h, m] = value.astype(jnp.bfloat16)
        done[h, m] = remote(out.at[h, m], inn.at[h, m], send.at[h, m], recv.at[h, m], on_z(way))

    def hops(h):
        for m in range(3):
            hop(h, m, ahead - h, pluses, plus_out, plus_in, plus_s, plus_r, 1)
            if h < behind:
                hop(h, m, h - behind, minuses, minus_out, minus_in, minus_s, minus_r, -1)

    homes = {}

    def send_home(q, block):
        (home_out if q else home_in)[q] = block.astype(jnp.bfloat16)
        if q:
            homes[q] = remote(home_out.at[q], home_in.at[q], home_s.at[q], home_r.at[q], on_a(-offsets[q]))

    def combine(g):
        lo, hi = parts[g]
        for j in range(1, line):
            backs[j, g].wait_recv()
        return dot_tn(picks[g], back_in[:, lo:hi].reshape(line * (hi - lo), dim + LANES))

    hops(0)
    early = combine(0)
    for q in range(holds[1][0]):
        send_home(q, early[q * tok : (q + 1) * tok])
    early = early[holds[1][0] * tok :]
    hops(1)
    late = combine(1)
    for q in list(range(holds[1][0] + 1, line)) + [holds[1][0]]:
        i = q - holds[1][0]
        block = late[i * tok : (i + 1) * tok]
        if q < holds[0][1]:
            block = block + early[i * tok : (i + 1) * tok]
        send_home(q, block)
    for h in range(2, ahead):
        hops(h)

    for q in range(1, line):
        homes[q].wait_recv()
    back = home_in[0].astype(jnp.float32)
    for q in range(1, line):
        back = back + home_in[q].astype(jnp.float32)
    dtok_ref[...] = back[:, 0:dim].astype(jnp.bfloat16)
    eye = (
        lax.broadcasted_iota(jnp.int32, (LANES, LANES), 0) == lax.broadcasted_iota(jnp.int32, (LANES, LANES), 1)
    ).astype(jnp.float32).astype(jnp.bfloat16)
    by_expert = dot_nt(eye, back[:, dim:].astype(jnp.bfloat16))
    expert_iota = lax.broadcasted_iota(jnp.int32, (LANES, tok), 0)
    chosen = [
        jnp.sum(jnp.where(expert_iota == ids_ref[k : k + 1, :], by_expert, 0.0), axis=0, keepdims=True)
        for k in range(top)
    ]
    dgate_ref[...] = (jnp.concatenate(chosen, axis=0) / gates_f).astype(jnp.bfloat16)

    for m, out_ref in enumerate((dwg_ref, dwu_ref, dwd_ref)):
        pluses[ahead - 1, m].wait_recv()
        minuses[behind - 1, m].wait_recv()
        out_ref[...] = (
            chip_sum(0, m) + plus_in[ahead - 1, m].astype(jnp.float32) + minus_in[behind - 1, m].astype(jnp.float32)
        )

    for copy in pending:
        copy.wait_send()


def hand_on(*refs):
    half = len(refs) // 2
    for source, target in zip(refs[:half], refs[half:]):
        target[...] = source[...]


def per_device(line, ring, cap, tokens, out_grad, expert_ids, gates, w_gate, w_up, w_down):
    tok, dim = tokens.shape
    top = expert_ids.shape[1]
    _, shard, hid = w_gate.shape
    slots = line * cap
    ahead, behind = ring // 2, ring - 1 - ring // 2
    bf16, f32 = jnp.bfloat16, jnp.float32
    dma = pltpu.SemaphoreType.DMA
    vmem = pl.BlockSpec(memory_space=pltpu.VMEM)
    shapes = [
        jax.ShapeDtypeStruct((tok, dim), bf16),
        jax.ShapeDtypeStruct((top, tok), bf16),
        jax.ShapeDtypeStruct((shard, hid), f32),
        jax.ShapeDtypeStruct((shard, hid), f32),
        jax.ShapeDtypeStruct((shard, hid), f32),
    ]
    results = pl.pallas_call(
        functools.partial(kernel, line, ring, cap),
        out_shape=shapes,
        in_specs=[vmem] * 7,
        out_specs=[vmem] * 5,
        scratch_shapes=[
            pltpu.VMEM((line, 2 * top, LANES), bf16),
            pltpu.VMEM((line, tok, 2 * dim), bf16),
            pltpu.VMEM((line, slots, 2 * dim), bf16),
            pltpu.VMEM((line, slots, 2 * dim), bf16),
            pltpu.VMEM((ring, 2, shard, 3 * hid), bf16),
            pltpu.VMEM((line, slots, 3 * hid), bf16),
            pltpu.VMEM((line, slots, dim + LANES), bf16),
            pltpu.VMEM((line, slots, dim + LANES), bf16),
            pltpu.VMEM((line, tok, dim + LANES), bf16),
            pltpu.VMEM((line, tok, dim + LANES), bf16),
            pltpu.VMEM((ring, 2, shard, 3 * hid), bf16),
            pltpu.VMEM((ring, shard, 3 * hid), bf16),
            pltpu.VMEM((ahead, 3, shard, hid), bf16),
            pltpu.VMEM((ahead, 3, shard, hid), bf16),
            pltpu.VMEM((behind, 3, shard, hid), bf16),
            pltpu.VMEM((behind, 3, shard, hid), bf16),
            dma((line,)), dma((line,)), dma((line, 2)), dma((line, 2)), dma((line, 2)), dma((line, 2)),
            dma((ring,)), dma((ring,)), dma((ring,)), dma((ring,)),
            dma((line, 2)), dma((line, 2)), dma((line,)), dma((line,)),
            dma((ring,)), dma((ring,)),
            dma((ahead, 3)), dma((ahead, 3)), dma((behind, 3)), dma((behind, 3)),
        ],
        compiler_params=pltpu.CompilerParams(
            collective_id=0, has_side_effects=True, vmem_limit_bytes=56 * 1024 * 1024
        ),
        name="expert_backward",
    )(tokens, out_grad, expert_ids.T, gates.T, w_gate[0], w_up[0], w_down[0])
    d_tokens, d_gates, d_gate_w, d_up_w, d_down_w = pl.pallas_call(
        hand_on, out_shape=shapes, in_specs=[vmem] * 5, out_specs=[vmem] * 5, name="hand_on"
    )(*results)
    return d_tokens, d_gates.T, d_gate_w[None], d_up_w[None], d_down_w[None]


def solution(mesh):
    experts, groups = mesh.shape["expert"], mesh.shape["dp"]
    line = 1
    while line * line < experts:
        line += 1
    split, both = P("expert", "dp", None), P(("expert", "dp"), None)

    def whole(tokens, out_grad, expert_ids, gates, w_gate, w_up, w_down):
        tok = tokens.shape[0] // (experts * groups)
        cap = max(2, 3 * tok * expert_ids.shape[1] // (2 * experts))
        return jax.shard_map(
            functools.partial(per_device, line, groups // 2, cap),
            mesh=mesh,
            in_specs=(both, both, both, both, split, split, split),
            out_specs=(both, both, split, split, split),
            check_vma=False,
        )(tokens, out_grad, expert_ids, gates, w_gate, w_up, w_down)

    return whole
```

time: 89.3 us -> 85.5 us (0.957)
  the two profiles are of different devices: /device:TPU:52 before, /device:TPU:32 now
where the time goes in v2:
time: 85.5 us; the launch traced here: 85.2 us
  Pallas kernels  84.6 us (99%)
    pallas_call x1, Pallas kernels, per_device(): pl.pallas_call(functools.partial(kernel, line, ring, cap), out_shape=shap...  82.8 us
    pallas_call x1, Pallas kernels, per_device(): pl.pallas_call(hand_on, out_shape=shapes, in_specs=[vmem] * 5, out_specs=...  1.76 us

profile of v2, /device:TPU:32, one launch (start us, length us, event | category | flops | bytes accessed | tf_op | source)
XLA Modules:
  0.0 85.2 jit_solution(3186686643812444078)
XLA Ops:
  0.6 82.8 %expert_backward.1 = (bf16[32,1024]{1,0:T(8,128)(2,1)}, bf16[8,32]{1,0:T(8,128)(2,1)}, f32[64,384]{1,0:T(8,128)}, f32[64,384]{1,0:T(8,128)}, f32[64,384]{1,0:T(8,128)}) custom-call(bf16[32,1024]{1,0:T(8,128)(2,1)} %tok_ref.1, bf16[32,1024]{1,0:T(8,128)(2,1)} %grad_ref.1, s32[8,32]{1,0:T(8,128)} %bitcast.12, bf16[8,32]{1,0:T(8,128)(2,1)} %bitcast.13, ...), custom_call_target="tpu_custom_call" | custom-call | tf_op jit(solution)/shard_map/expert_backward/pallas_call | solution.py:362
  83.5 1.8 %hand_on.1 = (bf16[32,1024]{1,0:T(8,128)(2,1)}, bf16[8,32]{1,0:T(8,128)(2,1)}, f32[64,384]{1,0:T(8,128)}, f32[64,384]{1,0:T(8,128)}, f32[64,384]{1,0:T(8,128)}) custom-call(bf16[32,1024]{1,0:T(8,128)(2,1)} %get-tuple-element.15.refs_0_, bf16[8,32]{1,0:T(8,128)(2,1)} %get-tuple-element.16.refs_1_, f32[64,384]{1,0:T(8,128)} %get-tuple-element.17.refs_2_, ...), custom_call_target="tpu_custom_call" | custom-call | tf_op jit(solution)/shard_map/hand_on/pallas_call | solution.py:395

commit v3 on v2

--- a/solution.py
+++ b/solution.py
@@ -24,7 +24,7 @@
 
 
 def split_rows(slots):
-    return (0, 16), (16, slots)
+    return [(lo, lo + 16) for lo in range(0, slots, 16)]
 
 
 def kernel(
@@ -118,8 +118,10 @@
         shared[k] = remote(ref, ref, ws_s.at[i], ws_r.at[i], sibling)
 
     near = (1, -1, 2, -2)
-    for k in near:
-        send_rows(place_of[k % line], 0, k)
+    halves = ((0, 2 * dim),)
+    for i, lanes in enumerate(halves):
+        for k in near:
+            send_rows(place_of[k % line], 0, k, i, lanes)
     for k in near:
         send_weights(k, 0, k)
     share(0)
@@ -144,7 +146,7 @@
     place = jnp.where(mask > 0.0, first + pos, -1.0)
     holds = [(lo // cap, -(-hi // cap)) for lo, hi in parts]
     slot_iota = lax.broadcasted_iota(jnp.int32, (slots, total), 0).astype(jnp.float32)
-    picks, scaled_picks = [[], []], [[], []]
+    picks, scaled_picks = [[] for _ in parts], [[] for _ in parts]
     for j in range(line):
         hit = slot_iota == place[j : j + 1]
         pick = jnp.where(hit, 1.0, 0.0)
@@ -166,24 +168,31 @@
             out = dot_nn(pick, held).astype(jnp.bfloat16)
             for j in range(line):
                 (send2 if j else recv2)[j, lo:hi, col : col + dim] = out[j * count : (j + 1) * count]
-        for q in range(1, line):
-            j = offsets[q]
+        for j in offsets[1:]:
             twos[j, g] = remote(
                 send2.at[j, lo:hi], recv2.at[j, lo:hi], two_s.at[j, g], two_r.at[j, g], on_b(j)
             )
 
-    for k in (1, -1):
-        ones[place_of[k % line], 0].wait_recv()
+    for i in range(len(halves)):
+        for k in (1, -1):
+            ones[place_of[k % line], i].wait_recv()
     dispatch(0)
-    for k in (2, -2):
-        ones[place_of[k % line], 0].wait_recv()
-    send_rows(place_of[3], place_of[2], 1)
-    send_rows(place_of[-3 % line], place_of[-2 % line], -1)
-    send_rows(place_of[4], place_of[2], 2, 0, (0, dim))
-    send_rows(place_of[4], place_of[-2 % line], -2, 1, (dim, 2 * dim))
-    for q, i in ((place_of[3], 0), (place_of[-3 % line], 0), (place_of[4], 0), (place_of[4], 1)):
-        ones[q, i].wait_recv()
+    for i, lanes in enumerate(halves):
+        for k in (2, -2):
+            ones[place_of[k % line], i].wait_recv()
+        send_rows(place_of[3], place_of[2], 1, i, lanes)
+        send_rows(place_of[-3 % line], place_of[-2 % line], -1, i, lanes)
+        if i == 0:
+            send_rows(place_of[4], place_of[2], 2, 0, (0, dim))
+        if i == len(halves) - 1:
+            send_rows(place_of[4], place_of[-2 % line], -2, 1, (dim, 2 * dim))
+    for i in range(len(halves)):
+        for k in (3, -3):
+            ones[place_of[k % line], i].wait_recv()
     dispatch(1)
+    for i in range(2):
+        ones[place_of[4], i].wait_recv()
+    dispatch(2)
 
     for k in near:
         weights[k].wait_recv()
@@ -233,12 +242,10 @@
                 back_out.at[j, lo:hi], back_in.at[j, lo:hi], back_s.at[j, g], back_r.at[j, g], on_b(-j)
             )
 
-    for j in range(1, line):
-        twos[j, 0].wait_recv()
-    expert_rows(0)
-    for j in range(1, line):
-        twos[j, 1].wait_recv()
-    expert_rows(1)
+    for g in range(len(parts)):
+        for j in range(1, line):
+            twos[j, g].wait_recv()
+        expert_rows(g)
 
     ahead, behind = ring // 2, ring - 1 - ring // 2
     targets = sorted(range(-behind, ahead + 1), key=lambda k: (-abs(k), -k))
@@ -293,19 +300,25 @@
             backs[j, g].wait_recv()
         return dot_tn(picks[g], back_in[:, lo:hi].reshape(line * (hi - lo), dim + LANES))
 
+    rest = {}
+
+    def settle(g):
+        out, (q0, q1) = combine(g), holds[g]
+        ready = holds[g + 1][0] if g + 1 < len(parts) else line
+        for q in sorted(range(q0, q1), key=lambda q: -q):
+            block = out[(q - q0) * tok : (q - q0 + 1) * tok]
+            if q in rest:
+                block = block + rest[q]
+            if q < ready:
+                send_home(q, block)
+            else:
+                rest[q] = block
+
     hops(0)
-    early = combine(0)
-    for q in range(holds[1][0]):
-        send_home(q, early[q * tok : (q + 1) * tok])
-    early = early[holds[1][0] * tok :]
+    settle(0)
+    settle(1)
     hops(1)
-    late = combine(1)
-    for q in list(range(holds[1][0] + 1, line)) + [holds[1][0]]:
-        i = q - holds[1][0]
-        block = late[i * tok : (i + 1) * tok]
-        if q < holds[0][1]:
-            block = block + early[i * tok : (i + 1) * tok]
-        send_home(q, block)
+    settle(2)
     for h in range(2, ahead):
         hops(h)
 
@@ -381,9 +394,9 @@
             pltpu.VMEM((ahead, 3, shard, hid), bf16),
             pltpu.VMEM((behind, 3, shard, hid), bf16),
             pltpu.VMEM((behind, 3, shard, hid), bf16),
-            dma((line,)), dma((line,)), dma((line, 2)), dma((line, 2)), dma((line, 2)), dma((line, 2)),
+            dma((line,)), dma((line,)), dma((line, 2)), dma((line, 2)), dma((line, 3)), dma((line, 3)),
             dma((ring,)), dma((ring,)), dma((ring,)), dma((ring,)),
-            dma((line, 2)), dma((line, 2)), dma((line,)), dma((line,)),
+            dma((line, 3)), dma((line, 3)), dma((line,)), dma((line,)),
             dma((ring,)), dma((ring,)),
             dma((ahead, 3)), dma((ahead, 3)), dma((behind, 3)), dma((behind, 3)),
         ],

time: 85.5 us -> 81.7 us (0.956)
  Pallas kernels: 84.6 us -> 80.8 us
    pallas_call x1, Pallas kernels: 82.8 us -> 79.1 us  [per_device(): pl.pallas_call(functools.partial(kernel, line, ring, cap), out_shape=shap...]
where the time goes in v3:
time: 81.7 us; the launch traced here: 81.5 us
  Pallas kernels  80.8 us (99%)
    pallas_call x1, Pallas kernels, per_device(): pl.pallas_call(functools.partial(kernel, line, ring, cap), out_shape=shap...  79.1 us
    pallas_call x1, Pallas kernels, per_device(): pl.pallas_call(hand_on, out_shape=shapes, in_specs=[vmem] * 5, out_specs=...  1.76 us

profile of v3, /device:TPU:32, one launch (start us, length us, event | category | flops | bytes accessed | tf_op | source)
XLA Modules:
  0.0 81.5 jit_solution(11530590433808115147)
XLA Ops:
  0.6 79.1 %expert_backward.1 = (bf16[32,1024]{1,0:T(8,128)(2,1)}, bf16[8,32]{1,0:T(8,128)(2,1)}, f32[64,384]{1,0:T(8,128)}, f32[64,384]{1,0:T(8,128)}, f32[64,384]{1,0:T(8,128)}) custom-call(bf16[32,1024]{1,0:T(8,128)(2,1)} %tok_ref.1, bf16[32,1024]{1,0:T(8,128)(2,1)} %grad_ref.1, s32[8,32]{1,0:T(8,128)} %bitcast.12, bf16[8,32]{1,0:T(8,128)(2,1)} %bitcast.13, ...), custom_call_target="tpu_custom_call" | custom-call | tf_op jit(solution)/shard_map/expert_backward/pallas_call | solution.py:375
  79.7 1.8 %hand_on.1 = (bf16[32,1024]{1,0:T(8,128)(2,1)}, bf16[8,32]{1,0:T(8,128)(2,1)}, f32[64,384]{1,0:T(8,128)}, f32[64,384]{1,0:T(8,128)}, f32[64,384]{1,0:T(8,128)}) custom-call(bf16[32,1024]{1,0:T(8,128)(2,1)} %get-tuple-element.15.refs_0_, bf16[8,32]{1,0:T(8,128)(2,1)} %get-tuple-element.16.refs_1_, f32[64,384]{1,0:T(8,128)} %get-tuple-element.17.refs_2_, ...), custom_call_target="tpu_custom_call" | custom-call | tf_op jit(solution)/shard_map/hand_on/pallas_call | solution.py:408

commit v4 on v3

--- a/solution.py
+++ b/solution.py
@@ -374,7 +374,7 @@
     ]
     results = pl.pallas_call(
         functools.partial(kernel, line, ring, cap),
-        out_shape=shapes,
+        out_shape=[pltpu.VMEM(s.shape, s.dtype) for s in shapes],
         in_specs=[vmem] * 7,
         out_specs=[vmem] * 5,
         scratch_shapes=[
@@ -401,12 +401,13 @@
             dma((ahead, 3)), dma((ahead, 3)), dma((behind, 3)), dma((behind, 3)),
         ],
         compiler_params=pltpu.CompilerParams(
-            collective_id=0, has_side_effects=True, vmem_limit_bytes=56 * 1024 * 1024
+            collective_id=0, has_side_effects=True, vmem_limit_bytes=54944 * 1024
         ),
         name="expert_backward",
     )(tokens, out_grad, expert_ids.T, gates.T, w_gate[0], w_up[0], w_down[0])
     d_tokens, d_gates, d_gate_w, d_up_w, d_down_w = pl.pallas_call(
-        hand_on, out_shape=shapes, in_specs=[vmem] * 5, out_specs=[vmem] * 5, name="hand_on"
+        hand_on, out_shape=shapes, in_specs=[vmem] * 5, out_specs=[vmem] * 5, name="hand_on",
+        compiler_params=pltpu.CompilerParams(vmem_limit_bytes=2 * 1024 * 1024),
     )(*results)
     return d_tokens, d_gates.T, d_gate_w[None], d_up_w[None], d_down_w[None]
 

time: 81.7 us -> 79.9 us (0.978)
  the two profiles are of different devices: /device:TPU:32 before, /device:TPU:64 now
where the time goes in v4:
time: 79.9 us; the launch traced here: 79.7 us
  Pallas kernels  79.1 us (99%)
    pallas_call x1, Pallas kernels, per_device(): pl.pallas_call(functools.partial(kernel, line, ring, cap), out_shape=[plt...  78.3 us

profile of v4, /device:TPU:64, one launch (start us, length us, event | category | flops | bytes accessed | tf_op | source)
XLA Modules:
  0.0 79.7 jit_solution(15575511061459271838)
XLA Ops:
  0.6 78.3 %expert_backward.1 = (bf16[32,1024]{1,0:T(8,128)(2,1)S(1)}, bf16[8,32]{1,0:T(8,128)(2,1)S(1)}, f32[64,384]{1,0:T(8,128)S(1)}, f32[64,384]{1,0:T(8,128)S(1)}, f32[64,384]{1,0:T(8,128)S(1)}) custom-call(bf16[32,1024]{1,0:T(8,128)(2,1)} %tok_ref.1, bf16[32,1024]{1,0:T(8,128)(2,1)} %grad_ref.1, s32[8,32]{1,0:T(8,128)} %bitcast.12, bf16[8,32]{1,0:T(8,128)(2,1)} %bitcast.13, ...), custom_call_target="tpu_custom_call" | custom-call | tf_op jit(solution)/shard_map/expert_backward/pallas_call | solution.py:375
  79.0 0.8 hand_on.1

commit v5 on v4

--- a/solution.py
+++ b/solution.py
@@ -32,7 +32,7 @@
     tok_ref, grad_ref, ids_ref, gates_ref, wg_ref, wu_ref, wd_ref,
     dtok_ref, dgate_ref, dwg_ref, dwu_ref, dwd_ref,
     meta, rows1, send2, recv2, wbuf, acts, back_out, back_in, home_out, home_in,
-    part, sib, plus_out, plus_in, minus_out, minus_in,
+    early, part, sib, plus_out, plus_in, minus_out, minus_in,
     meta_s, meta_r, one_s, one_r, two_s, two_r, w_s, w_r, ws_s, ws_r,
     back_s, back_r, home_s, home_r, sib_s, sib_r, plus_s, plus_r, minus_s, minus_r,
 ):
@@ -242,24 +242,38 @@
                 back_out.at[j, lo:hi], back_in.at[j, lo:hi], back_s.at[j, g], back_r.at[j, g], on_b(-j)
             )
 
+    ahead, behind = ring // 2, ring - 1 - ring // 2
+    targets = sorted(range(-behind, ahead + 1), key=lambda k: (-abs(k), -k))
+
+    def weight_grads(k, lo, hi):
+        at = z_at(k) * (2 * shard)
+        cut = pl.ds(pl.multiple_of(at, 2 * shard), 2 * shard)
+        cut_grad = pl.ds(pl.multiple_of(dim + at, 2 * shard), 2 * shard)
+        count = line * (hi - lo)
+        pair = acts[:, lo:hi, 0 : 2 * hid].reshape(count, 2 * hid)
+        hidden = acts[:, lo:hi, 2 * hid :].reshape(count, hid)
+        return (
+            dot_tn(recv2[:, lo:hi, cut].reshape(count, 2 * shard), pair),
+            dot_tn(recv2[:, lo:hi, cut_grad].reshape(count, 2 * shard), hidden),
+        )
+
     for g in range(len(parts)):
         for j in range(1, line):
             twos[j, g].wait_recv()
         expert_rows(g)
-
-    ahead, behind = ring // 2, ring - 1 - ring // 2
-    targets = sorted(range(-behind, ahead + 1), key=lambda k: (-abs(k), -k))
-    pair_grad = acts[:, :, 0 : 2 * hid].reshape(line * slots, 2 * hid)
-    hidden = acts[:, :, 2 * hid :].reshape(line * slots, hid)
+        if g == 0:
+            for i, k in enumerate(targets):
+                pair, down = weight_grads(k, *parts[0])
+                early[i, :, 0 : 2 * hid] = pair
+                early[i, :, 2 * hid :] = down
+
     sibs = {}
     for i, k in enumerate(targets):
-        zt = z_at(k)
-        cut = pl.ds(pl.multiple_of(zt * (2 * shard), 2 * shard), 2 * shard)
-        cut_grad = pl.ds(pl.multiple_of(dim + zt * (2 * shard), 2 * shard), 2 * shard)
-        cols_in = recv2[:, :, cut].reshape(line * slots, 2 * shard)
-        cols_scaled = recv2[:, :, cut_grad].reshape(line * slots, 2 * shard)
-        part[i, :, :, 0 : 2 * hid] = dot_tn(cols_in, pair_grad).astype(jnp.bfloat16).reshape(2, shard, 2 * hid)
-        part[i, :, :, 2 * hid :] = dot_tn(cols_scaled, hidden).astype(jnp.bfloat16).reshape(2, shard, hid)
+        pair, down = weight_grads(k, parts[1][0], slots)
+        pair = (pair + early[i, :, 0 : 2 * hid]).astype(jnp.bfloat16)
+        down = (down + early[i, :, 2 * hid :]).astype(jnp.bfloat16)
+        part[i, :, :, 0 : 2 * hid] = pair.reshape(2, shard, 2 * hid)
+        part[i, :, :, 2 * hid :] = down.reshape(2, shard, hid)
         sibs[k] = remote(part.at[i, 1 - c], sib.at[i], sib_s.at[i], sib_r.at[i], sibling)
 
     met = set()
@@ -388,6 +402,7 @@
             pltpu.VMEM((line, slots, dim + LANES), bf16),
             pltpu.VMEM((line, tok, dim + LANES), bf16),
             pltpu.VMEM((line, tok, dim + LANES), bf16),
+            pltpu.VMEM((ring, 2 * shard, 3 * hid), f32),
             pltpu.VMEM((ring, 2, shard, 3 * hid), bf16),
             pltpu.VMEM((ring, shard, 3 * hid), bf16),
             pltpu.VMEM((ahead, 3, shard, hid), bf16),

time: 79.9 us -> 80 us (level)
  the two profiles are of different devices: /device:TPU:64 before, /device:TPU:32 now
where the time goes in v5:
time: 80 us; the launch traced here: 79.8 us
  Pallas kernels  79.1 us (99%)
    pallas_call x1, Pallas kernels, per_device(): pl.pallas_call(functools.partial(kernel, line, ring, cap), out_shape=[plt...  78.4 us

profile of v5, /device:TPU:32, one launch (start us, length us, event | category | flops | bytes accessed | tf_op | source)
XLA Modules:
  0.0 79.8 jit_solution(17975882985484655179)
XLA Ops:
  0.6 78.4 %expert_backward.1 = (bf16[32,1024]{1,0:T(8,128)(2,1)S(1)}, bf16[8,32]{1,0:T(8,128)(2,1)S(1)}, f32[64,384]{1,0:T(8,128)S(1)}, f32[64,384]{1,0:T(8,128)S(1)}, f32[64,384]{1,0:T(8,128)S(1)}) custom-call(bf16[32,1024]{1,0:T(8,128)(2,1)} %tok_ref.1, bf16[32,1024]{1,0:T(8,128)(2,1)} %grad_ref.1, s32[8,32]{1,0:T(8,128)} %bitcast.12, bf16[8,32]{1,0:T(8,128)(2,1)} %bitcast.13, ...), custom_call_target="tpu_custom_call" | custom-call | tf_op jit(solution)/shard_map/expert_backward/pallas_call | solution.py:389
  79.0 0.8 hand_on.1
